TPU v7x, 512 devices: a whole 4x8x8 slice. The times are simulated.
512 devices in a mesh: row: 8 (over z_lo, core), col: 8 (over z_hi, x), freq: 8 (over y).
Axes of the slice: x: 4, y: 8, z: 8 (z_hi: 2, z_lo: 4; z = z_hi * 4 + z_lo), core: 2. Of those that a mesh axis runs over, the one named last changes fastest.
Arguments:
- voltages: bfloat16 [16, 4096, 1024], P('freq', ('row', 'col')), may hold values from -6 to 6
- pair_owner: int32 [136], replicated, may hold values from 0 to 3
- chan_level: int32 [16], P('freq'), may hold values from 0 to 7
- stencil_table: float32 [4, 8, 3], replicated, may hold values from 0.2 to 1
Outputs:
- smoothed: float32 [16, 2, 8, 64, 8, 4096], P('freq', None, None, ('row', 'col'))
All inputs are finite; a program needn't handle non-finite values.
Results may differ from a plain program's by a relative error of at most 0.0003.
Values may be sent and summed in bfloat16 or wider, within the bound.
A program may use at most 64 MiB of HBM per device.

v0:
```python
import jax
import jax.numpy as jnp
from jax import lax
from jax.sharding import PartitionSpec as P


def from_root(value, axis, source):
    kept = jnp.where(lax.axis_index(axis) == source, value, 0).astype(value.dtype)
    return lax.psum(kept, axis)


def with_halo(cells, sides, width):
    for axis, dim in sides:
        count = lax.axis_size(axis)
        ends = count - 1
        head = lax.slice_in_dim(cells, 0, width, axis=dim)
        tail = lax.slice_in_dim(cells, cells.shape[dim] - width, cells.shape[dim], axis=dim)
        cells = jnp.concatenate(
            [
                lax.ppermute(tail, axis, [(i, (i + 1) % count) for i in range(ends)]),
                cells,
                lax.ppermute(head, axis, [((i + 1) % count, i) for i in range(ends)]),
            ],
            axis=dim,
        )
    return cells


def owner_grid(pair_owner, tiles):
    across = lax.broadcasted_iota(jnp.int32, (tiles, tiles), 0)
    downto = lax.broadcasted_iota(jnp.int32, (tiles, tiles), 1)
    lower_tile = jnp.minimum(across, downto)
    upper_tile = jnp.maximum(across, downto)
    position = lower_tile * tiles - lower_tile * (lower_tile - 1) // 2 + upper_tile - lower_tile
    slots_all = jnp.arange(pair_owner.shape[0], dtype=jnp.int32)
    matches = position[:, :, None] == slots_all[None, None, :]
    return jnp.sum(jnp.where(matches, pair_owner[None, None, :], 0), axis=2)


def correlate(row_part, col_part, time_scale):
    samples = row_part.shape[-1] // 2
    turned = jnp.concatenate([row_part[..., samples:], -row_part[..., :samples]], axis=-1)
    stacked = jnp.stack([row_part, turned], axis=1)
    product = jnp.einsum("fapt,fqt->fapq", stacked, col_part, preferred_element_type=jnp.float32)
    return product * time_scale


def adjoint(tile_pair):
    parity = jnp.array([1.0, -1.0], jnp.float32).reshape(1, 2, 1, 1)
    return jnp.swapaxes(tile_pair, 2, 3) * parity


def deliver(payload, row_count, col_count):
    dims_now = payload.shape
    spread = dims_now[:3] + (row_count, col_count) + dims_now[4:]
    arrived = lax.all_to_all(payload, ("row", "col"), split_axis=3, concat_axis=3, tiled=True)
    arrived = arrived.reshape(spread)
    return arrived


def on_device(voltages, pair_owner, chan_level, stencil_table):
    channels = voltages.shape[0]
    samples = voltages.shape[2] // 2
    time_scale = 1.0 / samples
    row_count = lax.axis_size("row")
    col_count = lax.axis_size("col")
    group_size = row_count * col_count
    row_index = lax.axis_index("row")
    col_index = lax.axis_index("col")
    row_panel = lax.all_gather(voltages, "col", axis=1, tiled=True)
    col_panel = from_root(row_panel, "row", col_index)
    block_width = row_panel.shape[1]
    half_width = block_width // 2
    stripe = block_width // group_size
    receiver = row_index * col_count + col_index
    half_index = receiver // (group_size // 2)
    empty_block = jnp.zeros((channels, 2, block_width, block_width), jnp.float32)
    full_block = lax.cond(
        row_index <= col_index,
        lambda: correlate(row_panel, col_panel, time_scale),
        lambda: empty_block,
    )
    mirrored = jnp.where(row_index < col_index, adjoint(full_block), 0.0)
    spread_rows = (channels, 2, group_size, stripe, block_width)
    payload = jnp.stack([full_block.reshape(spread_rows), mirrored.reshape(spread_rows)], axis=1)
    arrived = deliver(payload, row_count, col_count)
    block_rows = lax.broadcasted_iota(jnp.int32, (row_count, col_count), 0)
    block_cols = lax.broadcasted_iota(jnp.int32, (row_count, col_count), 1)
    keep_own = (block_rows <= block_cols)[None, None, :, :, None, None]
    own_part = arrived[:, 0]
    mirror_part = jnp.swapaxes(arrived[:, 1], 2, 3)
    merged = jnp.transpose(jnp.where(keep_own, own_part, mirror_part), (0, 1, 2, 4, 3, 5))
    assembled = merged.reshape(channels, 2, row_count, stripe, col_count, 2, half_width)
    tile_count = 2 * row_count
    owner_table = owner_grid(pair_owner, tile_count).astype(jnp.float32)
    row_select = (
        2 * lax.broadcasted_iota(jnp.int32, (row_count, tile_count), 0) + half_index
        == lax.broadcasted_iota(jnp.int32, (row_count, tile_count), 1)
    ).astype(jnp.float32)
    row_owner = jnp.dot(row_select, owner_table, precision=lax.Precision.HIGHEST)
    owner_hot = (
        row_owner.reshape(row_count, col_count, 2)[..., None]
        == jnp.arange(stencil_table.shape[0], dtype=jnp.float32)
    ).astype(jnp.float32)
    level_hot = (
        chan_level[:, None] == jnp.arange(stencil_table.shape[1], dtype=jnp.int32)[None, :]
    ).astype(jnp.float32)
    tap_weights = jnp.einsum(
        "fl,bdts,slk->fkbdt", level_hot, owner_hot, stencil_table, precision=lax.Precision.HIGHEST
    )
    padded = with_halo(assembled, (("freq", 0),), 1)
    weight_prev = tap_weights[:, 0][:, None, :, None, :, :, None]
    weight_here = tap_weights[:, 1][:, None, :, None, :, :, None]
    weight_next = tap_weights[:, 2][:, None, :, None, :, :, None]
    filtered = (
        weight_prev * padded[0:channels]
        + weight_here * padded[1 : channels + 1]
        + weight_next * padded[2 : channels + 2]
    )
    return filtered.reshape(channels, 2, row_count, 1, stripe, col_count * block_width)


def solution(mesh):
    in_specs = (P("freq", ("row", "col"), None), P(), P("freq"), P())
    out_specs = P("freq", None, None, ("row", "col"), None, None)
    return jax.shard_map(
        on_device, mesh=mesh, in_specs=in_specs, out_specs=out_specs, check_vma=False
    )
```

profile of v0, /device:TPU:1, one launch (start us, length us, event | category | flops | bytes accessed | tf_op | source)
XLA Modules:
  0.0 490.9 jit_solution(7453488248966553254)
XLA Ops:
  6.5 0.7 all-gather.2.cloned.1.call-update
  7.3 89.6 %all-gather.2.cloned.1.call-done = bf16[2,512,1024]{2,1,0:T(8,128)(2,1)} async-done(((bf16[2,64,1024]{2,1,0:T(8,128)(2,1)}), bf16[2,512,1024]{2,1,0:T(8,128)(2,1)}) %all-gather.2.cloned.1.call-update) | async-done | bytes 2097168 | tf_op jit(solution)/shard_map/all_gather | solution.py:70
  96.9 1.5 broadcast_select_fusion
  98.4 83.2 %all-reduce.2.cloned.1.call-done = bf16[2,512,1024]{2,1,0:T(8,128)(2,1)} async-done(((bf16[2,512,1024]{2,1,0:T(8,128)(2,1)}), bf16[2,512,1024]{2,1,0:T(8,128)(2,1)}) %all-reduce.2.cloned.1.call-update) | async-done | bytes 2097168 | tf_op jit(solution)/shard_map/psum | solution.py:9
  181.6 5.0 %conditional.1 = (f32[2,1,2,64,8,512]{5,4,3,2,0,1:T(8,128)}, f32[2,2,512,512]{2,3,1,0:T(8,128)}) conditional(s32[]{:T(128)} %convert_element_type.12, () %tuple.15, (bf16[2,512,1024]{2,1,0:T(8,128)(2,1)S(1)}, bf16[2,512,1024]{2,1,0:T(8,128)(2,1)}) %tuple.30), branch_computations={%region_2.3_spmd, %region_3.4_spmd} | conditional | flops 2155347968 | bytes 35651628 | solution.py:78
  181.6 2.5 broadcast_in_dim.25.clone
  184.1 2.5 stack_reshape.7
  186.7 2.8 select_bitcast_fusion
  189.4 3.5 pad_maximum_fusion
  193.0 4.3 copy.48
  197.2 16.9 %all-to-all-start = ((f32[2,2,2,64,8,512]{5,4,2,0,1,3:T(8,128)}), f32[2,2,2,64,8,512]{5,4,2,0,1,3:T(8,128)}, u32[]{:S(2)}, u32[]{:S(2)}) async-start(f32[2,2,2,64,8,512]{5,4,2,0,1,3:T(8,128)} %copy.48), calls=%async_computation | async-start | bytes 16777216 | tf_op jit(solution)/shard_map/all_to_all | solution.py:56
  214.2 182.1 %all-to-all-done = f32[2,2,2,64,8,512]{5,4,2,0,1,3:T(8,128)} async-done(((f32[2,2,2,64,8,512]{5,4,2,0,1,3:T(8,128)}), f32[2,2,2,64,8,512]{5,4,2,0,1,3:T(8,128)}, u32[]{:S(2)}, u32[]{:S(2)}) %all-to-all-start) | async-done | bytes 8388640 | tf_op jit(solution)/shard_map/all_to_all | solution.py:56
  396.3 4.5 fusion.38
  400.9 8.2 %fusion.14 = f32[2,2,8,8,8,512]{5,4,3,2,1,0:T(8,128)S(1)} fusion(f32[2,1,2,8,8,8,512]{6,5,2,0,1,4,3:T(8,128)S(1)} %get-tuple-element.21, f32[2,1,2,8,8,8,512]{6,5,2,0,1,4,3:T(8,128)S(1)} %get-tuple-element.20, pred[8,8]{1,0:T(8,128)(4,1)S(1)} %iota_compare_fusion.2), kind=kLoop, calls=%fused_computation.18 | loop fusion | flops 1048576 | bytes 12582976 | tf_op jit(solution)/shard_map/transpose | solution.py:92
  409.1 2.1 fusion.39
  411.1 0.6 copy-done.1
  411.7 3.6 slice.45
  415.3 4.5 collective-permute-start
  419.7 2.4 slice.50
  422.1 1.5 collective-permute-start.1
  423.7 0.4 select_reduce_fusion
  424.1 0.2 fusion.28
  424.4 0.2 convolution_bitcast_fusion.1
  424.7 0.2 convolution_bitcast_fusion
  424.9 0.2 copy.46
  425.1 0.2 copy.51
  425.2 0.2 copy.52
  425.4 5.9 %reshape.58 = f32[2,2,8,8,8,2,256]{6,5,4,3,2,1,0:T(2,128)} reshape(f32[2,2,8,8,8,512]{5,4,3,2,1,0:T(8,128)} %copy-done.1) | data formatting | bytes 8388608 | tf_op jit(solution)/shard_map/reshape | solution.py:93
  431.3 29.1 %collective-permute-done = f32[1,2,8,8,8,2,256]{6,5,4,3,2,1,0:T(2,128)} collective-permute-done((f32[1,2,8,8,8,2,256]{6,5,4,3,2,1,0:T(2,128)}, f32[1,2,8,8,8,2,256]{6,5,4,3,2,1,0:T(2,128)}, u32[]{:S(2)}, u32[]{:S(2)}) %collective-permute-start) | collective-permute-done | bytes 2097184 | tf_op jit(solution)/shard_map/ppermute | solution.py:20
  460.4 7.5 %collective-permute-done.1 = f32[1,2,8,8,8,2,256]{6,5,4,3,2,1,0:T(2,128)S(1)} collective-permute-done((f32[1,2,8,8,8,2,256]{6,5,4,3,2,1,0:T(2,128)}, f32[1,2,8,8,8,2,256]{6,5,4,3,2,1,0:T(2,128)S(1)}, u32[]{:S(2)}, u32[]{:S(2)}) %collective-permute-start.1) | collective-permute-done | bytes 2097184 | tf_op jit(solution)/shard_map/ppermute | solution.py:22
  467.9 9.8 %fusion.10 = f32[2,2,8,8,8,2,256]{6,5,4,3,2,1,0:T(2,128)} fusion(f32[1,2,8,8,8,2,256]{6,5,4,3,2,1,0:T(2,128)S(1)} %collective-permute-done.1, f32[2,2,8,8,8,2,256]{6,5,4,3,2,1,0:T(2,128)} %reshape.58, f32[1,2,8,8,8,2,256]{6,5,4,3,2,1,0:T(2,128)} %collective-permute-done, f32[2,8,8,2]{3,2,1,0:T(8,128)S(1)} %copy.52, f32[2,8,8,2]{3,2,1,0:T(8,128)S(1)} %copy.51, ...), kind=kLoop, calls=%fused_computation.12 | loop fusion | flops 7340032 | bytes 12585984 | tf_op jit(solution)/shard_map/add | solution.py:116
  477.7 6.4 %reshape.59 = f32[2,2,8,1,8,4096]{5,4,2,1,0,3:T(8,128)} reshape(f32[2,2,8,8,8,2,256]{6,5,4,3,2,1,0:T(2,128)} %fusion.10) | data formatting | bytes 8388608 | tf_op jit(solution)/shard_map/reshape | solution.py:120
  (19 shorter events, 0.2 us)
Async XLA Ops:
  6.5 417.9 %copy-start = (f32[4,8,3]{1,0,2:T(4,128)S(1)}, f32[4,8,3]{1,0,2:T(4,128)}, u32[]{:S(2)}) copy-start(f32[4,8,3]{1,0,2:T(4,128)} %param.10) | copy-start | bytes 1156
  6.5 90.3 %all-gather.2.cloned.1.call-start = ((), (), s32[]{:S(2)}) async-start(), calls=%async_computation.1 | async-start | bytes 2359296 | tf_op jit(solution)/shard_map/all_gather | solution.py:70
  7.3 174.4 %all-reduce.2.cloned.1.call-start = ((), (), s32[]{:S(2)}) async-start(), calls=%async_computation.2 | async-start | bytes 4194304 | tf_op jit(solution)/shard_map/psum | solution.py:9
  96.9 84.7 %copy-start.2 = (bf16[2,512,1024]{2,1,0:T(8,128)(2,1)S(1)}, bf16[2,512,1024]{2,1,0:T(8,128)(2,1)}, u32[]{:S(2)}) copy-start(bf16[2,512,1024]{2,1,0:T(8,128)(2,1)} %all-gather.2.cloned.1.call-done) | copy-start | bytes 6291460
  181.6 5.0 %copy-start.4 = (f32[2]{0:T(128)S(1)}, f32[2]{0:T(128)}, u32[]{:S(2)}) copy-start(f32[2]{0:T(128)} %constant.55.clone) | copy-start | bytes 28
  197.2 199.1 %all-to-all-start = ((f32[2,2,2,64,8,512]{5,4,2,0,1,3:T(8,128)}), f32[2,2,2,64,8,512]{5,4,2,0,1,3:T(8,128)}, u32[]{:S(2)}, u32[]{:S(2)}) async-start(f32[2,2,2,64,8,512]{5,4,2,0,1,3:T(8,128)} %copy.48), calls=%async_computation | async-start | bytes 16777216 | tf_op jit(solution)/shard_map/all_to_all | solution.py:56
  409.0 2.6 copy-start.1
  411.7 12.0 %copy-start.3 = (s32[136]{0:T(256)S(1)}, s32[136]{0:T(256)}, u32[]{:S(2)}) copy-start(s32[136]{0:T(256)} %param.8) | copy-start | bytes 1636
  411.7 12.7 %copy-start.6 = (s32[2]{0:T(128)S(1)}, s32[2]{0:T(128)}, u32[]{:S(2)}) copy-start(s32[2]{0:T(128)} %param.9) | copy-start | bytes 28
  415.3 45.2 %collective-permute-start = (f32[1,2,8,8,8,2,256]{6,5,4,3,2,1,0:T(2,128)}, f32[1,2,8,8,8,2,256]{6,5,4,3,2,1,0:T(2,128)}, u32[]{:S(2)}, u32[]{:S(2)}) collective-permute-start(f32[1,2,8,8,8,2,256]{6,5,4,3,2,1,0:T(2,128)} %slice.45), channel_id=1, source_target_pairs={{0,1},{1,2},{2,3},{3,4},{4,5},{5,6},{6,7},{8,9},{9,10},{10,11},{11... | collective-permute-start | bytes 6291464 | tf_op jit(solution)/shard_map/ppermute | solution.py:20
  422.1 45.8 %collective-permute-start.1 = (f32[1,2,8,8,8,2,256]{6,5,4,3,2,1,0:T(2,128)}, f32[1,2,8,8,8,2,256]{6,5,4,3,2,1,0:T(2,128)S(1)}, u32[]{:S(2)}, u32[]{:S(2)}) collective-permute-start(f32[1,2,8,8,8,2,256]{6,5,4,3,2,1,0:T(2,128)} %slice.50), channel_id=1, source_target_pairs={{1,0},{2,1},{3,2},{4,3},{5,4},{6,5},{7,6},{9,8},{10,9},{11,10},{12... | collective-permute-start | bytes 6291464 | tf_op jit(solution)/shard_map/ppermute | solution.py:22
Sparse Core Ops, SparseCore 0:
  10.6 86.2 all-gather.1
  99.8 81.7 all-reduce.1
where the time goes:
time: 500 us; the launch traced here: 491 us
  waiting for transfers between devices  392 us (78%)
  local copies, waits for them, and re-layouts  35.4 us (7%)
  other arithmetic  26.1 us (5%)
  starting transfers between devices  22.9 us (5%)
  between operations  13.5 us (3%)
    all_to_all x1, waiting for transfers between devices, deliver(): lax.all_to_all(payload, ('row', 'col'), split_axis=3, concat_axis=3, tile...  182 us
    all_gather x1, waiting for transfers between devices, on_device(): row_panel = lax.all_gather(voltages, 'col', axis=1, tiled=True)  89.6 us
    psum x1, waiting for transfers between devices, from_root(): return lax.psum(kept, axis)  83.2 us
    ppermute x1, waiting for transfers between devices, with_halo(): lax.ppermute(tail, axis, [(i, (i + 1) % count) for i in range(ends)])  29.1 us
    all_to_all x1, starting transfers between devices, deliver(): lax.all_to_all(payload, ('row', 'col'), split_axis=3, concat_axis=3, tile...  16.9 us
  transfers between devices with their start and end apart: 5, of which 5 were waited for; matrix products, arithmetic and copies ran while one was open for 2% of the time, Pallas kernels for 0%

commit v1 on v0

v1 whole, which is shorter than its diff:
```python
import jax
import jax.numpy as jnp
from jax import lax
from jax.experimental import pallas as pl
from jax.experimental.pallas import tpu as pltpu
from jax.sharding import PartitionSpec as P

MESH = pl.DeviceIdType.MESH
FULL = 32760.0
FINE = 128.0
PAD = 16
SHARD = 64
UNIT = 2 * SHARD


def correlator_kernel(
    v_ref, owner_ref, level_ref, table_ref, out_ref,
    vb, stripes, rows_own, rows_mate, a2, gram, smooth, hsend, hrecv, psend, precv,
    rows_s, rows_r, mate_s, mate_r, z_s, z_r, x_s, x_r, d_s, d_r, h_s, h_r, p_s, p_r,
):
    row, col, freq = lax.axis_index("row"), lax.axis_index("col"), lax.axis_index("freq")
    freq_count = lax.axis_size("freq")
    core, z_lo = row % 2, row // 2
    x, z_hi = col % 4, col // 4
    z = z_hi * 4 + z_lo
    side = x // 2

    def at_z(there):
        return ((there % 4) * 2 + core, (there // 4) * 4 + x, freq)

    z_next, z_prev = at_z((z + 1) % 8), at_z((z + 7) % 8)
    x_mate = (row, z_hi * 4 + (x + 1 - 2 * (x % 2)), freq)
    p_mate = (row, z_hi * 4 + (x + 3 + 2 * (x % 2)) % 4, freq)
    sibling = (row + 1 - 2 * core, col, freq)
    f_next = (row, col, (freq + 1) % freq_count)
    f_prev = (row, col, (freq + freq_count - 1) % freq_count)
    diagonal = row == col

    own_half = pl.multiple_of((x % 2) * SHARD, SHARD)
    mate_half = pl.multiple_of((1 - x % 2) * SHARD, SHARD)

    def remote(src, dst, send, recv, device):
        return pltpu.make_async_remote_copy(
            src_ref=src, dst_ref=dst, send_sem=send, recv_sem=recv,
            device_id=device, device_id_type=MESH,
        )

    def row_copy(c):
        return remote(stripes.at[c], rows_own.at[row], rows_s.at[c], rows_r.at[row], (col, c, freq))

    def row_arrival(b):
        return remote(stripes.at[0], rows_own.at[b], rows_s.at[0], rows_r.at[b], (b, row, freq))

    def mate_copy():
        return remote(rows_own, rows_mate, mate_s.at[0], mate_r.at[0], p_mate)

    def z_copy(way, stream, t):
        before = (t - 1) if way == 0 else (9 - t) % 8
        after = t if way == 0 else 8 - t
        ch = 1 if stream == 2 else 0
        start, size = (mate_half if stream == 1 else own_half), SHARD
        first = 0
        if stream == 2 and t == 4:
            first, size = way * (SHARD // 2), SHARD // 2
        if t == 1 and stream != 1:
            src = v_ref.at[ch]
        else:
            src = vb.at[before, ch, pl.ds(start + first, size)]
        dst = vb.at[after, ch, pl.ds(start + first, size)]
        return remote(
            src, dst, z_s.at[way, stream, t - 1], z_r.at[way, stream, t - 1],
            z_next if way == 0 else z_prev,
        )

    def x_copy(d, ch):
        slot = 8 if ch == 0 else d
        src = v_ref.at[ch] if d == 0 else vb.at[d, ch, pl.ds(own_half, SHARD)]
        return remote(src, vb.at[d, ch, pl.ds(own_half, SHARD)], x_s.at[slot], x_r.at[slot], x_mate)

    def x_arrival(d, ch):
        slot = 8 if ch == 0 else d
        here = vb.at[d, ch, pl.ds(mate_half, SHARD)]
        return remote(here, here, x_s.at[slot], x_r.at[slot], x_mate)

    def d_copy(d, ch):
        return remote(
            vb.at[d, ch, pl.ds(0, UNIT)], vb.at[d, ch, pl.ds(UNIT, UNIT)],
            d_s.at[d, ch], d_r.at[d, ch], sibling,
        )

    def h_copy(d, ch):
        return remote(
            hsend.at[d, ch], hrecv.at[d, ch], h_s.at[d, ch], h_r.at[d, ch],
            f_prev if ch == 0 else f_next,
        )

    def p_copy(d):
        return remote(psend.at[d], precv.at[d], p_s.at[d], p_r.at[d], p_mate)

    def encode(source, target, top):
        step = jnp.ceil(FINE * jnp.log(jnp.maximum(top, 1e-36)))
        inverse = jnp.exp(step * (-1.0 / FINE))
        for r in range(0, 256, 32):
            value = source[pl.ds(r, 32), :]
            share = jnp.minimum(jnp.abs(value) * inverse, 1.0)
            root = share * lax.rsqrt(share + 1e-30) * FULL
            code = jnp.where(value < 0, -root, root)
            target[pl.ds(r, 32), :] = jnp.round(code).astype(jnp.int32).astype(jnp.int16)
        target[pl.ds(256, PAD), :] = jnp.broadcast_to(step, (PAD, 256)).astype(jnp.int32).astype(jnp.int16)

    def scale_of(message, lanes):
        step = message[pl.ds(256, PAD), lanes].astype(jnp.int32).astype(jnp.float32)
        return jnp.exp(step * (1.0 / FINE)) * (1.0 / (FULL * FULL))

    def decoded(message, r, lanes):
        code = message[pl.ds(r, 16), lanes].astype(jnp.int32).astype(jnp.float32)
        return code * jnp.abs(code)

    def fill_rows(source, dev):
        wide = source[...].astype(jnp.float32)
        for ch in range(2):
            part = wide[:, 8 * ch : 8 * ch + 8, :].reshape(64, 1024).astype(jnp.bfloat16)
            base = dev * 128
            a2[ch, base : base + 64, :] = part
            a2[ch, base + 64 : base + 128, :512] = part[:, 512:]
            a2[ch, base + 64 : base + 128, 512:] = -part[:, :512]

    def products(d):
        for ch in range(2):
            d_copy(d, ch).wait_recv()
        for ch in range(2):
            g = lax.dot_general(
                a2[ch], vb[d, ch], (((1,), (1,)), ((), ())), preferred_element_type=jnp.float32
            )
            gram[d, ch] = g
            encode(gram.at[d, ch], hsend.at[d, ch], jnp.max(jnp.abs(g), keepdims=True))
            h_copy(d, ch).start()

    def place(d, cr):
        there = (z - d + 8) % 8
        block = (there % 4) * 2 + (core if cr == 0 else 1 - core)
        return block, there // 4

    def smoothing(d):
        for ch in range(2):
            h_copy(d, ch).wait_recv()
        top = jnp.zeros((16, 128), jnp.float32)
        for cr in range(2):
            lanes = pl.ds(cr * UNIT, UNIT)
            block, high = place(d, cr)
            first = pl.multiple_of(block * 512 + high * 256 + side * UNIT, UNIT)
            tile = block * 2 + high
            scale_next = scale_of(hrecv.at[d, 0], lanes)
            scale_prev = scale_of(hrecv.at[d, 1], lanes)
            for pair in range(4):
                taps = []
                for b in (2 * pair, 2 * pair + 1):
                    mine = 2 * b + row // 4
                    low = jnp.minimum(mine, tile)
                    spot = low * 16 - low * (low - 1) // 2 + jnp.abs(mine - tile)
                    owner = owner_ref[spot]
                    taps.append(
                        [[table_ref[owner, level_ref[ch], k] * (1.0 / 512) for k in range(3)] for ch in range(2)]
                    )
                wide = [
                    [
                        jnp.concatenate(
                            [jnp.full((8, 128), taps[0][ch][k]), jnp.full((8, 128), taps[1][ch][k])], axis=0
                        )
                        for k in range(3)
                    ]
                    for ch in range(2)
                ]
                wide_prev = jnp.where(freq > 0, wide[0][0] * scale_prev, 0.0)
                wide_next = jnp.where(freq < freq_count - 1, wide[1][2] * scale_next, 0.0)
                for dev in range(2):
                    for part in range(2):
                        r = (dev * 2 + part) * 64 + pair * 16
                        g0 = gram[d, 0, pl.ds(r, 16), lanes]
                        g1 = gram[d, 1, pl.ds(r, 16), lanes]
                        before = decoded(hrecv.at[d, 1], r, lanes)
                        after = decoded(hrecv.at[d, 0], r, lanes)
                        f0 = wide_prev * before + wide[0][1] * g0 + wide[0][2] * g1
                        f1 = wide[1][0] * g0 + wide[1][1] * g1 + wide_next * after
                        if dev == 0:
                            for ch, value in ((0, f0), (1, f1)):
                                out_ref[ch, part, 2 * pair : 2 * pair + 2, 0, :, pl.ds(first, UNIT)] = (
                                    value.reshape(2, 8, 128)
                                )
                        else:
                            for ch, value in ((0, f0), (1, f1)):
                                smooth[pl.ds((ch * 2 + part) * 64 + pair * 16, 16), lanes] = value
                            top = jnp.maximum(top, jnp.maximum(jnp.abs(f0), jnp.abs(f1)))
        encode(smooth, psend.at[d], jnp.max(top, keepdims=True))
        p_copy(d).start()

    def delivery(d):
        p_copy(d).wait_recv()
        for cr in range(2):
            lanes = pl.ds(cr * UNIT, UNIT)
            block, high = place(d, cr)
            first = pl.multiple_of(block * 512 + high * 256 + (1 - side) * UNIT, UNIT)
            scale = scale_of(precv.at[d], lanes)
            for ch in range(2):
                for part in range(2):
                    for pair in range(4):
                        value = decoded(precv.at[d], (ch * 2 + part) * 64 + pair * 16, lanes) * scale
                        out_ref[ch, part, 2 * pair : 2 * pair + 2, 0, :, pl.ds(first, UNIT)] = (
                            value.reshape(2, 8, 128)
                        )

    barrier = pltpu.get_barrier_semaphore()
    for device in (z_next, z_prev, x_mate, p_mate, sibling, f_next, f_prev):
        pl.semaphore_signal(barrier, inc=1, device_id=device, device_id_type=MESH)
    for other in range(8):
        for device in ((col, other, freq), (other, row, freq)):
            @pl.when(jnp.logical_not(jnp.logical_and(device[0] == row, device[1] == col)))
            def _():
                pl.semaphore_signal(barrier, inc=1, device_id=device, device_id_type=MESH)

    narrow = v_ref[...]
    wide_v = narrow.astype(jnp.float32)
    for c in range(8):
        pieces = [wide_v[ch, 8 * c : 8 * c + 8, :] for ch in range(2)]
        stripes[c] = jnp.concatenate(pieces, axis=0).astype(jnp.bfloat16)
    for ch in range(2):
        vb[0, ch, pl.ds(own_half, SHARD), :] = narrow[ch]

    pl.semaphore_wait(barrier, 23 - 2 * jnp.where(diagonal, 1, 0))

    for c in range(8):
        @pl.when(jnp.logical_not(jnp.logical_and(diagonal, c == col)))
        def _():
            row_copy(c).start()

    @pl.when(diagonal)
    def _():
        rows_own[row] = stripes[col]

    x_copy(0, 0).start()
    for way in range(2):
        z_copy(way, 0, 1).start()
    x_copy(0, 1).start()
    for way in range(2):
        z_copy(way, 2, 1).start()

    x_arrival(0, 0).wait_recv()
    for way in range(2):
        z_copy(way, 1, 1).start()
    d_copy(0, 0).start()
    x_arrival(0, 1).wait_recv()
    d_copy(0, 1).start()

    for b in range(8):
        @pl.when(jnp.logical_not(jnp.logical_and(diagonal, b == row)))
        def _():
            row_arrival(b).wait_recv()
    mate_copy().start()
    fill_rows(rows_own, 0)
    mate_copy().wait_recv()
    fill_rows(rows_mate, 1)

    ready, smoothed = [0], []
    for t in range(1, 5):
        here = [t, 8 - t] if t < 4 else [4]
        for stream in range(3):
            ways = [0, 1]
            if t == 4 and stream < 2:
                ways = [stream]
            for way in ways:
                z_copy(way, stream, t).wait_recv()
                if t < 3 or (t == 3 and (stream == 2 or way == stream)):
                    z_copy(way, stream, t + 1).start()
            if stream == 0:
                for d in ready:
                    products(d)
            elif stream == 1:
                for d in here:
                    d_copy(d, 0).start()
                for d in smoothed:
                    delivery(d)
            else:
                for d in here:
                    x_copy(d, 1).start()
                for d in ready:
                    smoothing(d)
                for d in here:
                    x_arrival(d, 1).wait_recv()
                    d_copy(d, 1).start()
        smoothed, ready = ready, here
    products(4)
    for d in smoothed:
        delivery(d)
    smoothing(4)
    delivery(4)

    for c in range(8):
        @pl.when(jnp.logical_not(jnp.logical_and(diagonal, c == col)))
        def _():
            row_copy(c).wait_send()
    mate_copy().wait_send()
    x_copy(0, 0).wait_send()
    for t in range(1, 5):
        for way in range(2):
            for stream in range(3):
                if t < 4 or stream == 2 or way == stream:
                    z_copy(way, stream, t).wait_send()
    for d in range(8):
        x_copy(d, 1).wait_send()
        p_copy(d).wait_send()
        for ch in range(2):
            d_copy(d, ch).wait_send()
            h_copy(d, ch).wait_send()


def on_device(voltages, pair_owner, chan_level, stencil_table):
    vmem = pl.BlockSpec(memory_space=pltpu.VMEM)
    smem = pl.BlockSpec(memory_space=pltpu.SMEM)
    dma = pltpu.SemaphoreType.DMA
    return pl.pallas_call(
        correlator_kernel,
        out_shape=jax.ShapeDtypeStruct((2, 2, 8, 1, 8, 4096), jnp.float32),
        in_specs=[vmem, smem, smem, smem],
        out_specs=vmem,
        scratch_shapes=[
            pltpu.VMEM((8, 2, 256, 1024), jnp.bfloat16),
            pltpu.VMEM((8, 16, 1024), jnp.bfloat16),
            pltpu.VMEM((8, 16, 1024), jnp.bfloat16),
            pltpu.VMEM((8, 16, 1024), jnp.bfloat16),
            pltpu.VMEM((2, 256, 1024), jnp.bfloat16),
            pltpu.VMEM((8, 2, 256, 256), jnp.float32),
            pltpu.VMEM((256, 256), jnp.float32),
            pltpu.VMEM((8, 2, 256 + PAD, 256), jnp.int16),
            pltpu.VMEM((8, 2, 256 + PAD, 256), jnp.int16),
            pltpu.VMEM((8, 256 + PAD, 256), jnp.int16),
            pltpu.VMEM((8, 256 + PAD, 256), jnp.int16),
            dma((8,)), dma((8,)), dma((1,)), dma((1,)),
            dma((2, 3, 4)), dma((2, 3, 4)),
            dma((9,)), dma((9,)),
            dma((8, 2)), dma((8, 2)),
            dma((8, 2)), dma((8, 2)),
            dma((8,)), dma((8,)),
        ],
        compiler_params=pltpu.CompilerParams(
            collective_id=0, has_side_effects=True, vmem_limit_bytes=44 * 1024 * 1024
        ),
    )(voltages, pair_owner, chan_level, stencil_table)


def solution(mesh):
    in_specs = (P("freq", ("row", "col"), None), P(), P("freq"), P())
    out_specs = P("freq", None, None, ("row", "col"), None, None)
    return jax.shard_map(
        on_device, mesh=mesh, in_specs=in_specs, out_specs=out_specs, check_vma=False
    )
```

time: 500 us -> 97.9 us (0.20); the launches traced: 491 us -> 97.7 us
  waiting for transfers between devices: 392 us -> 0 us
  Pallas kernels: 0 us -> 92.6 us
  local copies, waits for them, and re-layouts: 35.4 us -> 5.08 us
  other arithmetic: 26.1 us -> 0 us
  starting transfers between devices: 22.9 us -> 0 us
  between operations: 13.5 us -> 0.01 us
    all_to_all x1 -> x0, waiting for transfers between devices: 182 us -> none  [deliver(): lax.all_to_all(payload, ('row', 'col'), split_axis=3, concat_axis=3, tile...]
    pallas_call x0 -> x1, Pallas kernels: none -> 92.6 us  [on_device(): pl.pallas_call(correlator_kernel, out_shape=jax.ShapeDtypeStruct((2, 2, 8...]
    all_gather x1 -> x0, waiting for transfers between devices: 89.6 us -> none  [on_device(): row_panel = lax.all_gather(voltages, 'col', axis=1, tiled=True)]
    psum x1 -> x0, waiting for transfers between devices: 83.2 us -> none  [from_root(): return lax.psum(kept, axis)]
    ppermute x2 -> x0, waiting for transfers between devices: 36.6 us -> none  [the longest x1 29.1 us: with_halo(): lax.ppermute(tail, axis, [(i, (i + 1) % count) for i in range(ends)])]
    all_to_all x1 -> x0, starting transfers between devices: 16.9 us -> none  [deliver(): lax.all_to_all(payload, ('row', 'col'), split_axis=3, concat_axis=3, tile...]
    slice x5 -> x0, local copies, waits for them, and re-layouts: 12.6 us -> none  [the longest x2 5.63 us: with_halo(): lax.slice_in_dim(cells, cells.shape[dim] - width, cells.shape[dim], axis=...]
    reshape x2 -> x0, local copies, waits for them, and re-layouts: 12.3 us -> none  [the longest x1 6.41 us: on_device(): filtered.reshape(channels, 2, row_count, 1, stripe, col_count * block_width)]
  transfers between devices with their start and end apart: 5 -> 0, of which waited for: 5 -> 0; matrix products, arithmetic and copies ran while one was open for 2% -> 0% of each run, Pallas kernels for 0% -> 0%
where the time goes in v1:
time: 97.9 us; the launch traced here: 97.7 us
  Pallas kernels  92.6 us (95%)
  local copies, waits for them, and re-layouts  5.08 us (5%)
    pallas_call x1, Pallas kernels, on_device(): pl.pallas_call(correlator_kernel, out_shape=jax.ShapeDtypeStruct((2, 2, 8...  92.6 us
    unnamed x8, local copies, waits for them, and re-layouts  5.08 us

profile of v1, /device:TPU:1, one launch (start us, length us, event | category | flops | bytes accessed | tf_op | source)
XLA Modules:
  0.0 97.7 jit_solution(839920383551817294)
XLA Ops:
  0.0 0.8 copy.5.table_ref
  0.8 0.0 copy-start
  0.8 0.9 copy-done
  1.7 0.0 copy-start.1
  1.7 0.7 copy-done.1
  2.4 0.0 copy-start.2
  2.4 0.7 copy-done.2
  3.1 92.6 %shard_map.46 = f32[2,2,8,1,8,4096]{5,4,3,2,1,0:T(8,128)S(1)} custom-call(bf16[2,64,1024]{2,1,0:T(8,128)(2,1)S(1)} %copy-done, s32[136]{0:T(256)S(1)} %copy-done.1, s32[2]{0:T(128)S(1)} %copy-done.2, f32[4,8,3]{2,1,0:T(8,128)S(1)} %copy.5.table_ref), custom_call_target="tpu_custom_call" | custom-call | tf_op jit(solution)/shard_map/pallas_call | solution.py:320
  95.7 2.0 %copy.7 = f32[2,2,8,1,8,4096]{5,4,3,2,1,0:T(8,128)} copy(f32[2,2,8,1,8,4096]{5,4,3,2,1,0:T(8,128)S(1)} %shard_map.46) | data formatting | bytes 8388608
Async XLA Ops:
  0.8 0.9 copy-start
  1.7 0.7 copy-start.1
  2.4 0.7 copy-start.2

commit v2 on v1

v2 whole, which is shorter than its diff:
```python
import jax
import jax.numpy as jnp
from jax import lax
from jax.experimental import pallas as pl
from jax.experimental.pallas import tpu as pltpu
from jax.sharding import PartitionSpec as P

MESH = pl.DeviceIdType.MESH
FULL = 32760.0
FINE = 128.0
PAD = 16
SHARD = 64
UNIT = 2 * SHARD
FIRST = "rxcav"
ORDER = (
    "I0 R0 C1 I1", "A1 B1 M0 g0", "X1 g1 C2 Y1", "A2 g7 f0 X2", "B2 f1 g2 C3", "Y2 g6 A3 f7", "X3 B3 f2 C4",
    "g3 Y3 f6 A4", "g5 B4 X4 o0", "o1 g4 f3 o7", "f5 o2 o6 f4", "o3 o5 o4",
)


def correlator_kernel(
    v_hbm, owner_hbm, level_hbm, table_hbm, out_ref,
    owner_ref, level_ref, table_ref, vb, stripes, rows_own, rows_mate, a2, gram, smooth, hsend, hrecv, psend, precv,
    in_s, rows_s, rows_r, mate_s, mate_r, z_s, z_r, x_s, x_r, d_s, d_r, h_s, h_r, p_s, p_r,
):
    row, col, freq = lax.axis_index("row"), lax.axis_index("col"), lax.axis_index("freq")
    freq_count = lax.axis_size("freq")
    core, z_lo = row % 2, row // 2
    x, z_hi = col % 4, col // 4
    z = z_hi * 4 + z_lo
    side = x // 2

    def at_z(there):
        return ((there % 4) * 2 + core, (there // 4) * 4 + x, freq)

    z_next, z_prev = at_z((z + 1) % 8), at_z((z + 7) % 8)
    x_mate = (row, z_hi * 4 + (x + 1 - 2 * (x % 2)), freq)
    p_mate = (row, z_hi * 4 + (x + 3 + 2 * (x % 2)) % 4, freq)
    sibling = (row + 1 - 2 * core, col, freq)
    f_next = (row, col, (freq + 1) % freq_count)
    f_prev = (row, col, (freq + freq_count - 1) % freq_count)
    diagonal = row == col

    own_half = pl.multiple_of((x % 2) * SHARD, SHARD)
    mate_half = pl.multiple_of((1 - x % 2) * SHARD, SHARD)

    def remote(src, dst, send, recv, device):
        return pltpu.make_async_remote_copy(
            src_ref=src, dst_ref=dst, send_sem=send, recv_sem=recv,
            device_id=device, device_id_type=MESH,
        )

    def row_copy(c):
        return remote(stripes.at[c], rows_own.at[row], rows_s.at[0], rows_r.at[row], (col, c, freq))

    def row_arrival(b):
        return remote(stripes.at[0], rows_own.at[b], rows_s.at[0], rows_r.at[b], (b, row, freq))

    def mate_copy(b):
        return remote(rows_own.at[b], rows_mate.at[b], mate_s.at[0], mate_r.at[0], p_mate)

    def z_copy(way, stream, t):
        before = (t - 1) if way == 0 else (9 - t) % 8
        after = t if way == 0 else 8 - t
        ch = 1 if stream == 2 else 0
        start, size = (mate_half if stream == 1 else own_half), SHARD
        first = 0
        if stream == 2 and t == 4:
            first, size = way * (SHARD // 2), SHARD // 2
        src = vb.at[before, ch, pl.ds(start + first, size)]
        dst = vb.at[after, ch, pl.ds(start + first, size)]
        return remote(
            src, dst, z_s.at[0], z_r.at[way, stream, t - 1],
            z_next if way == 0 else z_prev,
        )

    def x_copy(d, ch):
        slot = 8 if ch == 0 else d
        part = vb.at[d, ch, pl.ds(own_half, SHARD)]
        return remote(part, part, x_s.at[0], x_r.at[slot], x_mate)

    def x_arrival(d, ch):
        slot = 8 if ch == 0 else d
        here = vb.at[d, ch, pl.ds(mate_half, SHARD)]
        return remote(here, here, x_s.at[0], x_r.at[slot], x_mate)

    def d_copy(d, ch, start):
        return remote(
            vb.at[d, ch, pl.ds(start, SHARD)], vb.at[d, ch, pl.ds(UNIT + start, SHARD)],
            d_s.at[0], d_r.at[d], sibling,
        )

    def d_arrival(d):
        here = vb.at[d, :, pl.ds(UNIT, UNIT)]
        return remote(here, here, d_s.at[0], d_r.at[d], sibling)

    def h_copy(d, ch, cr):
        return remote(
            hsend.at[d, cr, ch], hrecv.at[d, cr, ch], h_s.at[0], h_r.at[d, cr],
            f_prev if ch == 0 else f_next,
        )

    def h_arrival(d, cr):
        return remote(hsend.at[d, cr], hrecv.at[d, cr], h_s.at[0], h_r.at[d, cr], f_next)

    def p_copy(d, cr):
        return remote(psend.at[d, cr], precv.at[d, cr], p_s.at[0], p_r.at[d], p_mate)

    def p_arrival(d):
        return remote(psend.at[d], precv.at[d], p_s.at[0], p_r.at[d], p_mate)

    def all_left():
        @pl.when(diagonal)
        def _():
            some = stripes.at[pl.ds(0, 7)]
            remote(some, some, rows_s.at[0], rows_r.at[0], sibling).wait_send()

        @pl.when(jnp.logical_not(diagonal))
        def _():
            remote(stripes, stripes, rows_s.at[0], rows_r.at[0], sibling).wait_send()

        for sent, semaphore in (
            (rows_own, mate_s),
            (vb.at[pl.ds(0, 7), 0, pl.ds(0, 3 * SHARD)], z_s),
            (vb.at[pl.ds(0, 3), 0, pl.ds(0, 3 * SHARD)], x_s),
            (vb.at[:, 0], d_s),
            (hsend, h_s),
            (psend, p_s),
        ):
            remote(sent, sent, semaphore.at[0], rows_r.at[0], sibling).wait_send()

    def encode(source, lanes, target, top):
        step = jnp.ceil(FINE * jnp.log(jnp.maximum(top, 1e-36)))
        inverse = jnp.exp(step * (-1.0 / FINE))
        for r in range(0, 256, 64):
            value = source[pl.ds(r, 64), lanes]
            share = jnp.minimum(jnp.abs(value) * inverse, 1.0)
            root = share * lax.rsqrt(share + 1e-30) * FULL
            code = jnp.where(value < 0, -root, root)
            target[pl.ds(r, 64), :] = jnp.round(code).astype(jnp.int32).astype(jnp.int16)
        target[pl.ds(256, PAD), :] = jnp.broadcast_to(step, (PAD, UNIT)).astype(jnp.int32).astype(jnp.int16)

    def scale_of(message):
        step = message[pl.ds(256, PAD), :].astype(jnp.int32).astype(jnp.float32)
        return jnp.exp(step * (1.0 / FINE)) * (1.0 / (FULL * FULL))

    def decoded(message, r):
        code = message[pl.ds(r, 16), :].astype(jnp.int32).astype(jnp.float32)
        return code * jnp.abs(code)

    def fill_rows(source, dev):
        wide = source[...].astype(jnp.float32)
        for ch in range(2):
            part = wide[:, 8 * ch : 8 * ch + 8, :].reshape(64, 1024).astype(jnp.bfloat16)
            base = dev * 128
            a2[ch, base : base + 64, :] = part
            a2[ch, base + 64 : base + 128, :512] = part[:, 512:]
            a2[ch, base + 64 : base + 128, 512:] = -part[:, :512]

    def products(d):
        d_arrival(d).wait_recv()
        tops = []
        for ch in range(2):
            g = lax.dot_general(
                a2[ch], vb[d, ch], (((1,), (1,)), ((), ())), preferred_element_type=jnp.float32
            )
            gram[d, ch] = g
            tops.append(jnp.max(jnp.abs(g), axis=0, keepdims=True))
        for cr in range(2):
            lanes = slice(cr * UNIT, (cr + 1) * UNIT)
            for ch in range(2):
                top = jnp.max(tops[ch][:, lanes], keepdims=True)
                encode(gram.at[d, ch], pl.ds(cr * UNIT, UNIT), hsend.at[d, cr, ch], top)
            for ch in range(2):
                h_copy(d, ch, cr).start()

    def place(d, cr):
        there = (z - d + 8) % 8
        block = (there % 4) * 2 + (core if cr == 0 else 1 - core)
        return block, there // 4

    def smoothing(d):
        for cr in range(2):
            h_arrival(d, cr).wait_recv()
            top = jnp.zeros((16, 128), jnp.float32)
            lanes = pl.ds(cr * UNIT, UNIT)
            block, high = place(d, cr)
            first = pl.multiple_of(block * 512 + high * 256 + side * UNIT, UNIT)
            tile = block * 2 + high
            scale_next = scale_of(hrecv.at[d, cr, 0])
            scale_prev = scale_of(hrecv.at[d, cr, 1])
            for pair in range(4):
                taps = []
                for b in (2 * pair, 2 * pair + 1):
                    mine = 2 * b + row // 4
                    low = jnp.minimum(mine, tile)
                    spot = low * 16 - low * (low - 1) // 2 + jnp.abs(mine - tile)
                    owner = owner_ref[spot]
                    taps.append(
                        [[table_ref[k, owner, level_ref[ch]] * (1.0 / 512) for k in range(3)] for ch in range(2)]
                    )
                wide = [
                    [
                        jnp.concatenate(
                            [jnp.full((8, 128), taps[0][ch][k]), jnp.full((8, 128), taps[1][ch][k])], axis=0
                        )
                        for k in range(3)
                    ]
                    for ch in range(2)
                ]
                wide_prev = jnp.where(freq > 0, wide[0][0] * scale_prev, 0.0)
                wide_next = jnp.where(freq < freq_count - 1, wide[1][2] * scale_next, 0.0)
                for dev in range(2):
                    for part in range(2):
                        r = (dev * 2 + part) * 64 + pair * 16
                        g0 = gram[d, 0, pl.ds(r, 16), lanes]
                        g1 = gram[d, 1, pl.ds(r, 16), lanes]
                        before = decoded(hrecv.at[d, cr, 1], r)
                        after = decoded(hrecv.at[d, cr, 0], r)
                        f0 = wide_prev * before + wide[0][1] * g0 + wide[0][2] * g1
                        f1 = wide[1][0] * g0 + wide[1][1] * g1 + wide_next * after
                        if dev == 0:
                            for ch, value in ((0, f0), (1, f1)):
                                out_ref[ch, part, 2 * pair : 2 * pair + 2, 0, :, pl.ds(first, UNIT)] = (
                                    value.reshape(2, 8, 128)
                                )
                        else:
                            for ch, value in ((0, f0), (1, f1)):
                                smooth[pl.ds((ch * 2 + part) * 64 + pair * 16, 16), :] = value
                            top = jnp.maximum(top, jnp.maximum(jnp.abs(f0), jnp.abs(f1)))
            encode(smooth, slice(None), psend.at[d, cr], jnp.max(top, keepdims=True))
            p_copy(d, cr).start()

    def delivery(d):
        p_arrival(d).wait_recv()
        for cr in range(2):
            block, high = place(d, cr)
            first = pl.multiple_of(block * 512 + high * 256 + (1 - side) * UNIT, UNIT)
            scale = scale_of(precv.at[d, cr])
            for ch in range(2):
                for part in range(2):
                    for pair in range(4):
                        value = decoded(precv.at[d, cr], (ch * 2 + part) * 64 + pair * 16) * scale
                        out_ref[ch, part, 2 * pair : 2 * pair + 2, 0, :, pl.ds(first, UNIT)] = (
                            value.reshape(2, 8, 128)
                        )

    fetches = [
        pltpu.make_async_copy(v_hbm.at[ch], vb.at[0, ch, pl.ds(own_half, SHARD)], in_s.at[ch]) for ch in range(2)
    ]
    fetches.append(pltpu.make_async_copy(owner_hbm, owner_ref, in_s.at[2]))
    fetches.append(pltpu.make_async_copy(level_hbm, level_ref, in_s.at[3]))
    fetches.append(pltpu.make_async_copy(table_hbm, table_ref, in_s.at[4]))
    for fetch in fetches:
        fetch.start()

    barrier = pltpu.get_barrier_semaphore()
    for device in (z_next, z_prev, x_mate, p_mate, sibling, f_next, f_prev):
        pl.semaphore_signal(barrier, inc=1, device_id=device, device_id_type=MESH)
    for turn in range(8):
        b = (col + 8 - turn) % 8

        @pl.when(jnp.logical_not(jnp.logical_and(diagonal, turn == 0)))
        def _():
            pl.semaphore_signal(barrier, inc=1, device_id=(b, row, freq), device_id_type=MESH)

    for fetch in fetches:
        fetch.wait()

    own = [vb[0, ch, pl.ds(own_half, SHARD), :].astype(jnp.float32) for ch in range(2)]
    for c in range(8):
        pieces = [own[ch][8 * c : 8 * c + 8, :] for ch in range(2)]
        stripes[c] = jnp.concatenate(pieces, axis=0).astype(jnp.bfloat16)

    pl.semaphore_wait(barrier, 15 - jnp.where(diagonal, 1, 0))

    @pl.when(diagonal)
    def _():
        rows_own[row] = stripes[col]

    for name in FIRST:
        if name == "r":
            for turn in range(8):
                c = (row + turn) % 8

                @pl.when(jnp.logical_not(jnp.logical_and(diagonal, turn == 0)))
                def _():
                    row_copy(c).start()
        elif name in "xv":
            x_copy(0, "xv".index(name)).start()
            d_copy(0, "xv".index(name), own_half).start()
        else:
            for way in range(2):
                z_copy(way, 0 if name == "a" else 2, 1).start()

    def units(t):
        return [t, 8 - t] if t < 4 else [4]

    def ring(stream, t):
        for way in range(2):
            if t < 4 or stream == 2 or way == stream:
                z_copy(way, stream, t).wait_recv()
                if t < 3 or (t == 3 and (stream == 2 or way == stream)):
                    z_copy(way, stream, t + 1).start()
                if t < 4 or stream < 2 or way == 1:
                    d = units(t)[way if t < 4 else 0]
                    if stream == 2:
                        x_copy(d, 1).start()
                    d_copy(d, stream // 2, mate_half if stream == 1 else own_half).start()

    def step(kind, t):
        if kind == "C":
            ring(2, t)
        elif kind == "A":
            ring(0, t)
        elif kind == "B":
            ring(1, t)
        elif kind in "XY":
            d = t if kind == "X" else 8 - t
            x_arrival(d, 1).wait_recv()
            d_copy(d, 1, mate_half).start()
        elif kind == "R":
            for turn in range(8):
                b = (col + 8 - turn) % 8

                @pl.when(jnp.logical_not(jnp.logical_and(diagonal, turn == 0)))
                def _():
                    row_arrival(b).wait_recv()
                mate_copy(b).start()
            fill_rows(rows_own, 0)
        elif kind == "M":
            remote(rows_own, rows_mate, mate_s.at[0], mate_r.at[0], p_mate).wait_recv()
            fill_rows(rows_mate, 1)
        elif kind == "I":
            x_arrival(0, t).wait_recv()
            if t == 0:
                for way in range(2):
                    z_copy(way, 1, 1).start()
            d_copy(0, t, mate_half).start()
        elif kind == "g":
            products(t)
        elif kind == "f":
            smoothing(t)
        elif kind == "o":
            delivery(t)

    for group in ORDER:
        for name in group.split():
            step(name[0], int(name[1]))
    all_left()


def on_device(voltages, pair_owner, chan_level, stencil_table):
    operands = (voltages, pair_owner, chan_level, jnp.transpose(stencil_table, (2, 0, 1)))
    anywhere = pl.BlockSpec(memory_space=pltpu.HBM)
    dma = pltpu.SemaphoreType.DMA
    return pl.pallas_call(
        correlator_kernel,
        out_shape=pltpu.VMEM((2, 2, 8, 1, 8, 4096), jnp.float32),
        in_specs=[anywhere] * 4,
        out_specs=pl.BlockSpec(memory_space=pltpu.VMEM),
        scratch_shapes=[
            pltpu.SMEM((136,), jnp.int32),
            pltpu.SMEM((2,), jnp.int32),
            pltpu.SMEM((3, 4, 8), jnp.float32),
            pltpu.VMEM((8, 2, 256, 1024), jnp.bfloat16),
            pltpu.VMEM((8, 16, 1024), jnp.bfloat16),
            pltpu.VMEM((8, 16, 1024), jnp.bfloat16),
            pltpu.VMEM((8, 16, 1024), jnp.bfloat16),
            pltpu.VMEM((2, 256, 1024), jnp.bfloat16),
            pltpu.VMEM((8, 2, 256, 256), jnp.float32),
            pltpu.VMEM((256, UNIT), jnp.float32),
            pltpu.VMEM((8, 2, 2, 256 + PAD, UNIT), jnp.int16),
            pltpu.VMEM((8, 2, 2, 256 + PAD, UNIT), jnp.int16),
            pltpu.VMEM((8, 2, 256 + PAD, UNIT), jnp.int16),
            pltpu.VMEM((8, 2, 256 + PAD, UNIT), jnp.int16),
            dma((5,)), dma((1,)), dma((8,)), dma((1,)), dma((1,)),
            dma((1,)), dma((2, 3, 4)),
            dma((1,)), dma((9,)),
            dma((1,)), dma((8,)),
            dma((1,)), dma((8, 2)),
            dma((1,)), dma((8,)),
        ],
        compiler_params=pltpu.CompilerParams(
            collective_id=0, has_side_effects=True, vmem_limit_bytes=44 * 1024 * 1024
        ),
    )(*(pltpu.with_memory_space_constraint(each, pltpu.HBM) for each in operands))


def solution(mesh):
    in_specs = (P("freq", ("row", "col"), None), P(), P("freq"), P())
    out_specs = P("freq", None, None, ("row", "col"), None, None)
    return jax.shard_map(
        on_device, mesh=mesh, in_specs=in_specs, out_specs=out_specs, check_vma=False
    )
```

time: 97.9 us -> 70.1 us (0.72)
  Pallas kernels: 92.6 us -> 67.1 us
  local copies, waits for them, and re-layouts: 5.08 us -> 2.02 us
    pallas_call x1, Pallas kernels: 92.6 us -> 67.1 us  [on_device(): pl.pallas_call(correlator_kernel, out_shape=pltpu.VMEM((2, 2, 8, 1, 8, 40...]
    unnamed x8 -> x1, local copies, waits for them, and re-layouts: 5.08 us -> 2.02 us
where the time goes in v2:
time: 70.1 us; the launch traced here: 69.1 us
  Pallas kernels  67.1 us (96%)
  local copies, waits for them, and re-layouts  2.02 us (3%)
    pallas_call x1, Pallas kernels, on_device(): pl.pallas_call(correlator_kernel, out_shape=pltpu.VMEM((2, 2, 8, 1, 8, 40...  67.1 us
    unnamed x1, local copies, waits for them, and re-layouts  2.02 us

profile of v2, /device:TPU:1, one launch (start us, length us, event | category | flops | bytes accessed | tf_op | source)
XLA Modules:
  0.0 69.1 jit_solution(9902958684466665294)
XLA Ops:
  0.0 67.1 %shard_map.46 = f32[2,2,8,1,8,4096]{5,4,3,2,1,0:T(8,128)S(1)} custom-call(bf16[2,64,1024]{2,1,0:T(8,128)(2,1)} %v_hbm.1, s32[136]{0:T(256)} %owner_hbm.1, s32[2]{0:T(128)} %level_hbm.1, f32[3,4,8]{2,1,0:T(4,128)} %bitcast.1), custom_call_target="tpu_custom_call" | custom-call | tf_op jit(solution)/shard_map/pallas_call | solution.py:357
  67.1 2.0 %copy.6 = f32[2,2,8,1,8,4096]{5,4,3,2,1,0:T(8,128)} copy(f32[2,2,8,1,8,4096]{5,4,3,2,1,0:T(8,128)S(1)} %shard_map.46) | data formatting | bytes 8388608
